TPU v7x, 512 devices: a whole 4x4x16 slice. The times are simulated.
512 devices in a mesh: stack: 64 (over x, z_lo, core), rows: 8 (over z_hi, y).
Axes of the slice: x: 4, y: 4, z: 16 (z_hi: 2, z_lo: 8; z = z_hi * 8 + z_lo), core: 2. Of those that a mesh axis runs over, the one named last changes fastest.
Arguments:
- interferograms: float32 [1024, 512, 1024], P('stack', 'rows'), may hold values from -48 to 48
- pairs: int32 [1024, 2], replicated, may hold values from 0 to 191, as said below
Outputs:
- filtered: float32 [192, 512, 1024], P('stack', 'rows')
Inputs may be any that keep to these rules, and one draw needn't show every extreme that they name: `pairs`: row k holds the reference date and then the secondary date of interferogram k, with reference < secondary <= reference + 24.
All inputs are finite; a program needn't handle non-finite values.
Results may differ from a plain program's by a relative error of at most 0.00007.
Values sent between devices are 32-bit elements; how exact they have to be, the bound alone decides.
A program may use at most 128 MiB of HBM per device.

v0:
```python
import jax
import jax.numpy as jnp
from jax import lax
from jax.sharding import PartitionSpec as P

ND = 192
R = 4


TIKHONOV = 0.1
TEMPORAL_SIGMA = 6.0
SPATIAL_SIGMA = 1.5


def with_halo(cells, sides, width):
    for axis, dim in sides:
        count = lax.axis_size(axis)
        ends = count - 1
        head = lax.slice_in_dim(cells, 0, width, axis=dim)
        tail = lax.slice_in_dim(cells, cells.shape[dim] - width, cells.shape[dim], axis=dim)
        cells = jnp.concatenate(
            [
                lax.ppermute(tail, axis, [(i, (i + 1) % count) for i in range(ends)]),
                cells,
                lax.ppermute(head, axis, [((i + 1) % count, i) for i in range(ends)]),
            ],
            axis=dim,
        )
    return cells


def build_tables(pairs, date_total):
    date_index = jnp.arange(date_total, dtype=jnp.int32)
    design = (pairs[:, 1:2] == date_index[None, :]).astype(jnp.float32) - (
        pairs[:, 0:1] == date_index[None, :]
    ).astype(jnp.float32)
    normal = jnp.dot(
        design.T, design, precision=lax.Precision.HIGHEST, preferred_element_type=jnp.float32
    )
    normal = normal + TIKHONOV * jnp.eye(date_total, dtype=jnp.float32)
    factor = jnp.linalg.cholesky(normal)
    pseudo = jax.scipy.linalg.cho_solve((factor, True), design.T)
    offsets = (date_index[:, None] - date_index[None, :]).astype(jnp.float32) / TEMPORAL_SIGMA
    kernel = jnp.exp(-0.5 * offsets * offsets)
    smooth = kernel / jnp.sum(kernel, axis=1, keepdims=True)
    return (pseudo, smooth)


def spatial_taps(radius):
    offsets = jnp.arange(-radius, radius + 1).astype(jnp.float32) / SPATIAL_SIGMA
    kernel = jnp.exp(-0.5 * offsets * offsets)
    return kernel / jnp.sum(kernel)


def along_rows(padded, height, weights):
    summed = weights[0] * padded[:, 0:height, :]
    for position in range(1, weights.shape[0]):
        summed = summed + weights[position] * padded[:, position : position + height, :]
    return summed


def along_columns(padded, length, weights):
    summed = weights[0] * padded[:, :, 0:length]
    for position in range(1, weights.shape[0]):
        summed = summed + weights[position] * padded[:, :, position : position + length]
    return summed


def shards(interferograms, pairs):
    pseudo, smooth = build_tables(pairs, ND)
    series = lax.all_to_all(interferograms, "stack", split_axis=1, concat_axis=0, tiled=True)
    series_depth = series.shape[0]
    middle_size = series.shape[1]
    inner_size = series.shape[2]
    flattened = series.reshape(series_depth, middle_size * inner_size)
    displacement = jnp.dot(
        pseudo, flattened, precision=lax.Precision.HIGHEST, preferred_element_type=jnp.float32
    )
    highpass = displacement - jnp.dot(
        smooth, displacement, precision=lax.Precision.HIGHEST, preferred_element_type=jnp.float32
    )
    date_field = lax.all_to_all(
        highpass.reshape(ND, middle_size, inner_size),
        "stack",
        split_axis=0,
        concat_axis=1,
        tiled=True,
    )
    weights = spatial_taps(R)
    padded = with_halo(date_field, (("rows", 1),), R)
    rowpass = along_rows(padded, date_field.shape[1], weights)
    widened = jnp.pad(rowpass, ((0, 0), (0, 0), (R, R)))
    return along_columns(widened, date_field.shape[2], weights)


def solution(mesh):
    return jax.shard_map(
        shards,
        mesh=mesh,
        in_specs=(P("stack", "rows", None), P()),
        out_specs=P("stack", "rows", None),
        check_vma=False,
    )
```

profile of v0, /device:TPU:24, one launch (start us, length us, event | category | flops | bytes accessed | tf_op | source)
XLA Modules:
  0.0 298.7 jit_solution(6949163043651453636)
XLA Ops:
  0.0 6.6 %copy.16 = f32[16,64,1024]{2,0,1:T(8,128)} copy(f32[16,64,1024]{2,1,0:T(8,128)} %param.2) | data formatting | bytes 8388608 | tf_op args[0]
  6.6 0.0 copy-start
  6.6 16.6 %all-to-all-start = ((f32[16,64,1024]{2,0,1:T(8,128)}), f32[16,64,1024]{2,0,1:T(8,128)}, u32[]{:S(2)}, u32[]{:S(2)}) async-start(f32[16,64,1024]{2,0,1:T(8,128)} %copy.16), calls=%async_computation | async-start | bytes 8388608 | tf_op jit(solution)/shard_map/all_to_all | solution.py:71
  23.2 0.0 copy-done
  23.2 2.4 fusion.1
  25.6 0.1 copy.15
  25.8 11.7 %cholesky.50 = f32[128,128]{1,0:T(8,128)S(1)} custom-call(f32[128,128]{1,0:T(8,128)S(1)} %cholesky.121), custom_call_target="Cholesky" | custom-call | tf_op jit(solution)/shard_map/jit(cholesky)/cholesky | solution.py:41
  37.6 9.8 %custom-call.18 = f32[1,128,128]{1,2,0:T(8,128)S(1)} custom-call(f32[1,128,128]{2,1,0:T(8,128)S(1)} %get-tuple-element.28), custom_call_target="InvertDiagBlocksLowerTriangular" | custom-call | tf_op jit(solution)/shard_map/jit(cholesky)/cholesky | solution.py:41
  47.4 0.2 constant_dynamic-update-slice_fusion.1
  47.6 0.2 convolution_subtract_fusion.3
  47.8 5.8 %cholesky.108 = f32[64,64]{1,0:T(8,128)S(1)} custom-call(f32[64,64]{1,0:T(8,128)S(1)} %convolution_subtract_fusion.3), custom_call_target="Cholesky" | custom-call | tf_op jit(solution)/shard_map/jit(cholesky)/cholesky | solution.py:41
  53.6 0.6 compare_reduce_fusion.1
  54.3 0.6 compare_reduce_fusion
  56.2 0.1 fusion.58
  56.3 19.7 %custom-call.19 = f32[2,128,128]{1,2,0:T(8,128)S(1)} custom-call(f32[2,128,128]{2,1,0:T(8,128)S(1)} %pad_maximum_fusion.2), custom_call_target="InvertDiagBlocksLowerTriangular" | custom-call | tf_op jit(solution)/shard_map/jit(_cho_solve)/triangular_solve | solution.py:42
  76.0 0.4 fusion.54
  76.4 0.1 convert_subtract_fusion
  76.5 0.6 fusion.47
  77.2 0.4 convolution_subtract_fusion.2
  77.6 0.4 fusion.64
  78.0 0.4 fusion.63
  78.4 0.6 convolution_subtract_fusion.1
  79.0 0.6 fusion.61
  79.6 125.6 %all-to-all-done = f32[16,64,1024]{2,0,1:T(8,128)} async-done(((f32[16,64,1024]{2,0,1:T(8,128)}), f32[16,64,1024]{2,0,1:T(8,128)}, u32[]{:S(2)}, u32[]{:S(2)}) %all-to-all-start) | async-done | bytes 4194336 | tf_op jit(solution)/shard_map/all_to_all | solution.py:71
  205.3 4.9 %fusion.43 = f32[192,1024]{1,0:T(8,128)S(1)} fusion(f32[1024,1024]{1,0:T(8,128)} %bitcast.12, f32[64,1024]{1,0:T(8,128)S(1)} %fusion.63, f32[128,1024]{1,0:T(8,128)S(1)} %fusion.61), kind=kOutput, calls=%fused_computation.71 | convolution fusion | flops 2416115712 | bytes 5767168 | tf_op jit(solution)/shard_map/dot_general | solution.py:76
  210.2 0.9 fusion
  211.1 1.7 copy.17
  212.7 11.9 %all-to-all-start.1 = ((f32[192,1,1024]{2,1,0:T(1,128)}), f32[192,1,1024]{2,1,0:T(1,128)S(1)}, u32[]{:S(2)}, u32[]{:S(2)}) async-start(f32[192,1,1024]{2,1,0:T(1,128)} %copy.17), calls=%async_computation.1 | async-start | bytes 1572864 | tf_op jit(solution)/shard_map/all_to_all | solution.py:82
  224.7 0.7 fusion.67
  225.4 0.7 broadcast_divide_fusion
  226.1 39.5 %all-to-all-done.1 = f32[192,1,1024]{2,1,0:T(1,128)S(1)} async-done(((f32[192,1,1024]{2,1,0:T(1,128)}), f32[192,1,1024]{2,1,0:T(1,128)S(1)}, u32[]{:S(2)}, u32[]{:S(2)}) %all-to-all-start.1) | async-done | bytes 786464 | tf_op jit(solution)/shard_map/all_to_all | solution.py:82
  265.6 0.1 copy.20
  265.8 2.7 collective-permute-start.1
  268.5 14.0 %collective-permute-start = (f32[3,4,1024]{2,1,0:T(4,128)S(1)}, f32[3,4,1024]{2,1,0:T(4,128)S(1)}, u32[]{:S(2)}, u32[]{:S(2)}) collective-permute-start(f32[3,4,1024]{2,1,0:T(4,128)S(1)} %get-tuple-element.25), channel_id=1, source_target_pairs={{0,1},{1,2},{2,3},{3,4},{4,5},{5,6},{6,7},{8,9},{9,10},{10,11},{11... | collective-permute-start | bytes 147464 | tf_op jit(solution)/shard_map/ppermute | solution.py:23
  282.5 0.7 fusion.73
  283.2 0.0 collective-permute-done.1
  283.2 1.0 collective-permute-done
  284.2 6.4 %fusion.24 = f32[3,64,1024]{2,1,0:T(8,128)S(1)} fusion(f32[3,64,1024]{2,1,0:T(8,128)S(1)} %bitcast.59, f32[3,4,1024]{2,1,0:T(4,128)S(1)} %collective-permute-done.1, f32[3,4,1024]{2,1,0:T(4,128)S(1)} %collective-permute-done, f32[]{:T(128)} %bitcast.24, f32[]{:T(128)} %bitcast.23, f32[]{:T(128)} %bitcast.22, f32[]{:T(128)} %bitcast.21, f32[]{:T(128)} %bitcast.20, ...), kind=kLoop, calls=%fused_computation.50 | loop fusion | flops 4915200 | bytes 1671204 | tf_op jit(solution)/shard_map/add | solution.py:58
  290.6 8.1 %fusion.13 = f32[3,64,1024]{2,1,0:T(8,128)} fusion(f32[3,64,1024]{2,1,0:T(8,128)S(1)} %fusion.24, f32[]{:T(128)} %bitcast.24, f32[]{:T(128)} %bitcast.23, f32[]{:T(128)} %bitcast.22, f32[]{:T(128)} %bitcast.21, f32[]{:T(128)} %bitcast.20, f32[]{:T(128)} %bitcast.19, f32[]{:T(128)} %bitcast.18, f32[]{:T(128)} %bitcast.17, f32[]{:T(128)} %bitcast), kind=kLoop, calls=%fused_computation.39 | loop fusion | flops 3342336 | bytes 1572900 | tf_op jit(solution)/shard_map/add | solution.py:65
  (12 shorter events, 0.2 us)
Async XLA Ops:
  6.6 16.6 %copy-start = (s32[1024,2]{0,1:T(2,128)S(1)}, s32[1024,2]{0,1:T(2,128)}, u32[]{:S(2)}) copy-start(s32[1024,2]{0,1:T(2,128)} %param.3) | copy-start | bytes 24580
  6.6 198.7 %all-to-all-start = ((f32[16,64,1024]{2,0,1:T(8,128)}), f32[16,64,1024]{2,0,1:T(8,128)}, u32[]{:S(2)}, u32[]{:S(2)}) async-start(f32[16,64,1024]{2,0,1:T(8,128)} %copy.16), calls=%async_computation | async-start | bytes 8388608 | tf_op jit(solution)/shard_map/all_to_all | solution.py:71
  212.7 52.9 %all-to-all-start.1 = ((f32[192,1,1024]{2,1,0:T(1,128)}), f32[192,1,1024]{2,1,0:T(1,128)S(1)}, u32[]{:S(2)}, u32[]{:S(2)}) async-start(f32[192,1,1024]{2,1,0:T(1,128)} %copy.17), calls=%async_computation.1 | async-start | bytes 1572864 | tf_op jit(solution)/shard_map/all_to_all | solution.py:82
  265.8 17.4 %collective-permute-start.1 = (f32[3,4,1024]{2,1,0:T(4,128)S(1)}, f32[3,4,1024]{2,1,0:T(4,128)S(1)}, u32[]{:S(2)}, u32[]{:S(2)}) collective-permute-start(f32[3,4,1024]{2,1,0:T(4,128)S(1)} %get-tuple-element.26), channel_id=1, source_target_pairs={{1,0},{2,1},{3,2},{4,3},{5,4},{6,5},{7,6},{9,8},{10,9},{11,10},{12... | collective-permute-start | bytes 147464 | tf_op jit(solution)/shard_map/ppermute | solution.py:25
  268.5 15.8 %collective-permute-start = (f32[3,4,1024]{2,1,0:T(4,128)S(1)}, f32[3,4,1024]{2,1,0:T(4,128)S(1)}, u32[]{:S(2)}, u32[]{:S(2)}) collective-permute-start(f32[3,4,1024]{2,1,0:T(4,128)S(1)} %get-tuple-element.25), channel_id=1, source_target_pairs={{0,1},{1,2},{2,3},{3,4},{4,5},{5,6},{6,7},{8,9},{9,10},{10,11},{11... | collective-permute-start | bytes 147464 | tf_op jit(solution)/shard_map/ppermute | solution.py:23
where the time goes:
time: 299 us
  waiting for transfers between devices  166 us (56%)
  other arithmetic  64.9 us (22%)
  starting transfers between devices  45.2 us (15%)
  matrix products  11.6 us (4%)
  local copies, waits for them, and re-layouts  9.27 us (3%)
    all_to_all x1, waiting for transfers between devices, shards(): lax.all_to_all(interferograms, 'stack', split_axis=1, concat_axis=0, tile...  126 us
    all_to_all x1, waiting for transfers between devices, shards(): lax.all_to_all(highpass.reshape(ND, middle_size, inner_size), 'stack', sp...  39.5 us
    another operation x7, other arithmetic, build_tables(): factor = jnp.linalg.cholesky(normal)  28.7 us
    another operation x6, other arithmetic, build_tables(): pseudo = jax.scipy.linalg.cho_solve((factor, True), design.T)  19.8 us
    all_to_all x1, starting transfers between devices, shards(): lax.all_to_all(interferograms, 'stack', split_axis=1, concat_axis=0, tile...  16.6 us
    ppermute x1, starting transfers between devices, with_halo(): lax.ppermute(tail, axis, [(i, (i + 1) % count) for i in range(ends)])  14 us
    all_to_all x1, starting transfers between devices, shards(): lax.all_to_all(highpass.reshape(ND, middle_size, inner_size), 'stack', sp...  11.9 us
    add x1, other arithmetic, along_columns(): summed + weights[position] * padded[:, :, position:position + length]  8.11 us
  transfers between devices with their start and end apart: 4, of which 3 were waited for; matrix products, arithmetic and copies ran while one was open for 19% of the time, Pallas kernels for 0%

commit v1 on v0

v1 whole, which is shorter than its diff:
```python
import functools

import jax
import jax.numpy as jnp
import numpy as np
from jax import lax
from jax.experimental import pallas as pl
from jax.experimental.pallas import tpu as pltpu
from jax.sharding import PartitionSpec as P

ND = 192
R = 4
TIKHONOV = 0.1
TEMPORAL_SIGMA = 6.0
SPATIAL_SIGMA = 1.5

LINE = 8
OWNERS = 8
DEPTH = 16
LANES = 128
CHUNKS = 8
SHARE = ND // LINE
KEEP = ND // (LINE * OWNERS)
PAD = 256
GROUP = 2
LAG = 3
ROUNDS = 9
f32 = jnp.float32
bf16 = jnp.bfloat16


def spatial_taps():
    offsets = np.arange(-R, R + 1).astype(np.float32) / np.float32(SPATIAL_SIGMA)
    taps = np.exp(np.float32(-0.5) * offsets * offsets)
    return [float(tap) for tap in (taps / np.sum(taps)).astype(np.float32)]


def dot(a, b):
    return jnp.dot(a, b, preferred_element_type=f32)


def two(a):
    high = a.astype(bf16)
    return high, (a - high.astype(f32)).astype(bf16)


def dot3(a, b):
    ah, al = two(a)
    bh, bl = two(b)
    return dot(ah, bh) + (dot(ah, bl) + dot(al, bh))


def dot6(a, b):
    return jnp.dot(a, b, precision=lax.Precision.HIGHEST, preferred_element_type=f32)


def inverse(normal, eye, ex):
    top = jnp.max(jnp.sum(jnp.abs(normal), axis=1, keepdims=True), axis=0, keepdims=True)
    scale = 2.0 / (top + TIKHONOV)
    ex[0:PAD] = eye - scale * normal
    ex[PAD : 2 * PAD] = scale * eye

    def turn(_, rho):
        both = ex[...]
        err = both[0:PAD]
        product = dot3(both, err)
        gain = 2.0 / (2.0 - rho * rho)
        ex[0:PAD] = gain * product[0:PAD] + (1.0 - gain) * eye
        ex[PAD : 2 * PAD] = gain * (both[PAD : 2 * PAD] + product[PAD : 2 * PAD])
        return 0.5 * rho * rho * gain

    lax.fori_loop(0, ROUNDS, turn, (top - TIKHONOV) / (top + TIKHONOV))

    def polish(_, carry):
        now = ex[PAD : 2 * PAD]
        left = eye - dot6(normal, now)
        ex[PAD : 2 * PAD] = now + dot3(now, left)
        return carry

    lax.fori_loop(0, 3, polish, 0)
    return ex[PAD : 2 * PAD]


def tables(z, pairs, ex, q_high, q_low):
    dates = lax.broadcasted_iota(jnp.int32, (PAD, pairs.shape[1]), 0)
    design = (dates == pairs[1:2, :]).astype(f32) - (dates == pairs[0:1, :]).astype(f32)
    design = design.astype(bf16)
    row = lax.broadcasted_iota(jnp.int32, (PAD, PAD), 0)
    col = lax.broadcasted_iota(jnp.int32, (PAD, PAD), 1)
    eye = (row == col).astype(f32)
    normal = lax.dot_general(design, design, (((1,), (1,)), ((), ())), preferred_element_type=f32)
    normal = normal + TIKHONOV * eye
    solved = inverse(normal, eye, ex)
    at_z = (row * 2731) >> 16
    rest = row - SHARE * at_z
    at_x = (rest * 43) >> 8
    date = 48 * at_x + 6 * at_z + (rest - 6 * at_x)
    offset = (date - col).astype(f32) / TEMPORAL_SIGMA
    weight = jnp.where(col < ND, jnp.exp(-0.5 * offset * offset), 0.0)
    smooth = weight / jnp.sum(weight, axis=1, keepdims=True)
    change = dot6((date == col).astype(f32) - smooth, solved)
    k = lax.broadcasted_iota(jnp.int32, (pairs.shape[1], LANES), 0)
    j = lax.broadcasted_iota(jnp.int32, (pairs.shape[1], LANES), 1)
    pick = (k == 256 * (j >> 5) + 32 * z + (j & 31)).astype(f32).astype(bf16)
    mine = dot(design, pick).astype(bf16)
    first = change.astype(bf16)
    rest = change - first.astype(f32)
    second = rest.astype(bf16)
    third = (rest - second.astype(f32)).astype(bf16)
    q = dot(first, mine) + (dot(second, mine) + dot(third, mine))
    high, low = two(q[0:ND])
    q_high[...] = jnp.concatenate([high, high], axis=1)
    q_low[...] = low


def kernel(
    ifg, pairs, out, x_buf, p_buf, r_buf, l_buf, fin, fr, ex, q_high, q_low,
    x_send, x_recv, r_send, r_recv, l_send, l_recv, f_send, f_recv, h_send, h_recv,
):
    stack = lax.axis_index("stack")
    slab = lax.axis_index("rows")
    slabs = lax.axis_size("rows")
    x = stack // (2 * LINE)
    z = (stack // 2) % LINE
    core = stack % 2
    me = 2 * x + core
    mirror = LINE - 1 - z
    half = z // (LINE // 2)
    near = z * (1 - half) + mirror * half
    wait_for = near + LAG * (LINE - 1 - near)

    def peer(owner):
        return {"stack": 2 * LINE * (owner // 2) + 2 * z + owner % 2}

    def remote(src, dst, send, recv, device):
        return pltpu.make_async_remote_copy(
            src_ref=src, dst_ref=dst, send_sem=send, recv_sem=recv,
            device_id=device, device_id_type=pl.DeviceIdType.MESH,
        )

    def landed(ref, sem):
        pltpu.make_async_copy(ref, ref, sem).wait()

    right = {"stack": stack + 2}
    left = {"stack": stack - 2}
    below = {"rows": slab + 1}
    above = {"rows": slab - 1}
    has_left, has_right = z > 0, z < LINE - 1
    has_above, has_below = slab > 0, slab < slabs - 1

    barrier = pltpu.get_barrier_semaphore()

    def greet(device):
        pl.semaphore_signal(barrier, inc=1, device_id=device, device_id_type=pl.DeviceIdType.MESH)

    for step in range(1, OWNERS):
        greet(peer((me + step) % OWNERS))
    for there, device in ((has_left, left), (has_right, right), (has_above, above), (has_below, below)):
        pl.when(there)(functools.partial(greet, device))
    count = OWNERS - 1 + (z + LINE - 1) // LINE + (mirror + LINE - 1) // LINE
    count = count + (slab + slabs - 1) // slabs + (2 * slabs - 2 - slab) // slabs
    pl.semaphore_wait(barrier, count)

    def x_piece(c, owner):
        rows = pl.ds(pl.multiple_of(8 * ((c + CHUNKS - 1) % CHUNKS), 8), 8)
        return ifg.at[:, rows, pl.ds(pl.multiple_of(LANES * owner, LANES), LANES)]

    def x_slot(c):
        return x_buf.at[c, pl.ds(DEPTH * me, DEPTH)]

    def spread(c, carry):
        for step in range(1, OWNERS):
            owner = (me + step) % OWNERS
            remote(x_piece(c, owner), x_slot(c), x_send.at[c], x_recv.at[c], peer(owner)).start()
        pltpu.make_async_copy(x_piece(c, me), x_slot(c), x_recv.at[c]).start()
        return carry

    lax.fori_loop(0, CHUNKS, spread, 0)

    tables(z, pairs, ex, q_high, q_low)

    @pl.when(jnp.logical_not(has_above))
    def _():
        fr[0] = jnp.zeros(fr.shape[1:], f32)

    @pl.when(jnp.logical_not(has_below))
    def _():
        fr[CHUNKS + 1] = jnp.zeros(fr.shape[1:], f32)

    taps = spatial_taps()

    def compute(c):
        landed(x_buf.at[c], x_recv.at[c])
        for s in range(0, 8, 2):
            block = jnp.concatenate([x_buf[c, :, s], x_buf[c, :, s + 1]], axis=1)
            high, low = two(block)
            product = dot(q_high[...], jnp.concatenate([high, low], axis=0)) + dot(q_low[...], high)
            for t in range(2):
                p_buf[c, :, s + t] = product[:, LANES * t : LANES * (t + 1)].reshape(LINE, SHARE, LANES)

    def collect(c):
        for s in range(8):
            fin[c, :, s] = p_buf[c, z, s]
        for step in range(1, OWNERS):
            owner = (me + step) % OWNERS
            remote(
                fin.at[c, pl.ds(KEEP * owner, KEEP)], fr.at[(c + CHUNKS - 1) % CHUNKS + 1, me],
                f_send.at[c], f_recv.at[c], peer(owner),
            ).start()
        pltpu.make_async_copy(
            fin.at[c, pl.ds(KEEP * me, KEEP)], fr.at[(c + CHUNKS - 1) % CHUNKS + 1, me], f_recv.at[c]
        ).start()

    def low_pass(q):
        lane = lax.broadcasted_iota(jnp.int32, (8, LANES * OWNERS), 1)
        for i in range(KEEP):
            window = jnp.concatenate(
                [fr[q, :, i, 8 - R : 8], fr[q + 1, :, i], fr[q + 2, :, i, 0:R]], axis=1
            )
            rowpass = taps[R] * window[:, R : R + 8]
            for s in range(1, R + 1):
                rowpass = rowpass + taps[R + s] * (
                    window[:, R - s : R - s + 8] + window[:, R + s : R + s + 8]
                )
            line = jnp.concatenate([rowpass[o] for o in range(OWNERS)], axis=1)
            total = taps[R] * line
            width = LANES * OWNERS
            for s in range(1, R + 1):
                before = jnp.where(lane >= s, pltpu.roll(line, s, 1), 0.0)
                after = jnp.where(lane < width - s, pltpu.roll(line, width - s, 1), 0.0)
                total = total + taps[R + s] * (before + after)
            out[i, pl.ds(pl.multiple_of(8 * q, 8), 8)] = total

    halo_down = remote(
        fr.at[CHUNKS, :, :, pl.ds(8 - R, R)], fr.at[0, :, :, pl.ds(8 - R, R)], h_send.at[0], h_recv.at[0], below
    )
    halo_up = remote(
        fr.at[1, :, :, pl.ds(0, R)], fr.at[CHUNKS + 1, :, :, pl.ds(0, R)], h_send.at[1], h_recv.at[1], above
    )

    def finish(c):
        landed(fr.at[(c + CHUNKS - 1) % CHUNKS + 1], f_recv.at[c])

        @pl.when((c == 0) & has_below)
        def _():
            halo_down.start()

        @pl.when((c == 1) & has_above)
        def _():
            halo_up.start()

        @pl.when(c >= 3)
        def _():
            low_pass(c - 2)

    span = (LINE - 1) * GROUP
    items = (LINE - 1) * CHUNKS

    def place(item):
        group = item // span
        rest = item % span
        return GROUP * group + rest % GROUP, rest // GROUP

    def step(t, carry):
        at = t - LAG * near

        @pl.when((at >= 0) & (at < items))
        def _():
            c, hop = place(at)

            @pl.when(hop == 0)
            def _():
                compute(c)

        at_right = t - LAG * z

        @pl.when((at_right >= 0) & (at_right < items))
        def _():
            c, hop = place(at_right)
            d = LINE - 1 - hop

            @pl.when((d >= z) & has_left)
            def _():
                landed(r_buf.at[c, d], r_recv.at[c, d])
                p_buf[c, d] = p_buf[c, d] + r_buf[c, d]

            @pl.when(d > z)
            def _():
                remote(p_buf.at[c, d], r_buf.at[c, d], r_send.at[c, d], r_recv.at[c, d], right).start()

        at_left = t - LAG * mirror

        @pl.when((at_left >= 0) & (at_left < items))
        def _():
            c, d = place(at_left)

            @pl.when((d <= z) & has_right)
            def _():
                landed(l_buf.at[c, d], l_recv.at[c, d])
                p_buf[c, d] = p_buf[c, d] + l_buf[c, d]

            @pl.when(d < z)
            def _():
                remote(p_buf.at[c, d], l_buf.at[c, d], l_send.at[c, d], l_recv.at[c, d], left).start()

        at_end = t - (GROUP * near + LAG * (LINE - 1 - near))

        @pl.when((at_end >= 0) & (at_end < items))
        def _():
            c, hop = place(at_end)

            @pl.when(hop == 0)
            def _():
                collect(c)

        at_out = at_end - LAG

        @pl.when((at_out >= 0) & (at_out < items))
        def _():
            c, hop = place(at_out)

            @pl.when(hop == 0)
            def _():
                finish(c)

        return carry

    steps = items + (LINE - 1) * max(LAG, GROUP) + LAG
    lax.fori_loop(0, steps, step, 0)

    @pl.when(has_above)
    def _():
        halo_down.wait_recv()
        halo_up.wait_send()

    @pl.when(has_below)
    def _():
        halo_up.wait_recv()
        halo_down.wait_send()

    def tail(q, carry):
        low_pass(q)
        return carry

    low_pass(0)
    lax.fori_loop(CHUNKS - 2, CHUNKS, tail, 0)

    def drain(c, carry):
        landed(x_buf.at[c, pl.ds(0, (OWNERS - 1) * DEPTH)], x_send.at[c])
        landed(fr.at[1, pl.ds(0, OWNERS - 1)], f_send.at[c])

        def each(d, carry):
            @pl.when(d > z)
            def _():
                landed(p_buf.at[c, d], r_send.at[c, d])

            @pl.when(d < z)
            def _():
                landed(p_buf.at[c, d], l_send.at[c, d])

            return carry

        return lax.fori_loop(0, LINE, each, carry)

    lax.fori_loop(0, CHUNKS, drain, 0)


def shards(interferograms, pairs):
    dma = pltpu.SemaphoreType.DMA
    block = (CHUNKS, LINE, 8, SHARE, LANES)
    return pl.pallas_call(
        kernel,
        out_shape=jax.ShapeDtypeStruct((KEEP,) + interferograms.shape[1:], f32),
        in_specs=[pl.BlockSpec(memory_space=pltpu.HBM), pl.BlockSpec(memory_space=pltpu.VMEM)],
        out_specs=pl.BlockSpec(memory_space=pltpu.VMEM),
        scratch_shapes=[
            pltpu.VMEM((CHUNKS, DEPTH * OWNERS, 8, LANES), f32),
            pltpu.VMEM(block, f32),
            pltpu.VMEM(block, f32),
            pltpu.VMEM(block, f32),
            pltpu.VMEM((CHUNKS, SHARE, 8, LANES), f32),
            pltpu.VMEM((CHUNKS + 2, OWNERS, KEEP, 8, LANES), f32),
            pltpu.VMEM((2 * PAD, PAD), f32),
            pltpu.VMEM((ND, 2 * LANES), bf16),
            pltpu.VMEM((ND, LANES), bf16),
            dma((CHUNKS,)), dma((CHUNKS,)),
            dma((CHUNKS, LINE)), dma((CHUNKS, LINE)),
            dma((CHUNKS, LINE)), dma((CHUNKS, LINE)),
            dma((CHUNKS,)), dma((CHUNKS,)),
            dma((2,)), dma((2,)),
        ],
        compiler_params=pltpu.CompilerParams(
            collective_id=0, has_side_effects=True, vmem_limit_bytes=48 * 1024 * 1024
        ),
    )(interferograms, pairs.T)


def solution(mesh):
    return jax.shard_map(
        shards,
        mesh=mesh,
        in_specs=(P("stack", "rows", None), P()),
        out_specs=P("stack", "rows", None),
        check_vma=False,
    )
```

time: 299 us -> 169 us (0.57)
  the two profiles are of different devices: /device:TPU:24 before, /device:TPU:25 now
where the time goes in v1:
time: 169 us; the launch traced here: 168 us
  Pallas kernels  165 us (98%)
  local copies, waits for them, and re-layouts  3.77 us (2%)
    pallas_call x1, Pallas kernels, shards(): pl.pallas_call(kernel, out_shape=jax.ShapeDtypeStruct((KEEP,) + interfero...  165 us
    unnamed x5, local copies, waits for them, and re-layouts  3.77 us

profile of v1, /device:TPU:25, one launch (start us, length us, event | category | flops | bytes accessed | tf_op | source)
XLA Modules:
  0.0 168.4 jit_solution(9803514030485973712)
XLA Ops:
  0.0 0.0 copy-start
  0.0 2.2 %copy-done = f32[16,64,1024]{2,1,0:T(8,128)S(1)} copy-done((f32[16,64,1024]{2,1,0:T(8,128)S(1)}, f32[16,64,1024]{2,1,0:T(8,128)}, u32[]{:S(2)}) %copy-start) | copy-done | bytes 4194328
  2.2 0.0 copy-start.1
  2.2 0.7 copy-done.1
  2.9 164.6 %shard_map.28 = f32[3,64,1024]{2,1,0:T(8,128)S(1)} custom-call(f32[16,64,1024]{2,1,0:T(8,128)S(1)} %copy-done, s32[2,1024]{1,0:T(2,128)S(1)} %bitcast.1), custom_call_target="tpu_custom_call" | custom-call | tf_op jit(solution)/shard_map/pallas_call | solution.py:371
  167.5 0.9 copy.4
Async XLA Ops:
  0.0 2.2 %copy-start = (f32[16,64,1024]{2,1,0:T(8,128)S(1)}, f32[16,64,1024]{2,1,0:T(8,128)}, u32[]{:S(2)}) copy-start(f32[16,64,1024]{2,1,0:T(8,128)} %ifg.1) | copy-start | bytes 12582916
  2.2 0.7 copy-start.1

commit v2 on v1

v2 whole, which is shorter than its diff:
```python
import functools

import jax
import jax.numpy as jnp
import numpy as np
from jax import lax
from jax.experimental import pallas as pl
from jax.experimental.pallas import tpu as pltpu
from jax.sharding import PartitionSpec as P

ND = 192
R = 4
TIKHONOV = 0.1
TEMPORAL_SIGMA = 6.0
SPATIAL_SIGMA = 1.5

LINE = 8
OWNERS = 8
DEPTH = 16
LANES = 128
BANDS = 8
CHUNKS = 16
HALF = 4
SHARE = ND // LINE
KEEP = ND // (LINE * OWNERS)
PAD = 256
WHOLE = 8
LAG = 6
AHEAD = 4
ROUNDS = 9
f32 = jnp.float32
bf16 = jnp.bfloat16


def spatial_taps():
    offsets = np.arange(-R, R + 1).astype(np.float32) / np.float32(SPATIAL_SIGMA)
    taps = np.exp(np.float32(-0.5) * offsets * offsets)
    return [float(tap) for tap in (taps / np.sum(taps)).astype(np.float32)]


def dot(a, b):
    return jnp.dot(a, b, preferred_element_type=f32)


def two(a):
    high = a.astype(bf16)
    return high, (a - high.astype(f32)).astype(bf16)


def dot3(a, b):
    ah, al = two(a)
    bh, bl = two(b)
    return dot(ah, bh) + (dot(ah, bl) + dot(al, bh))


def dot6(a, b):
    return jnp.dot(a, b, precision=lax.Precision.HIGHEST, preferred_element_type=f32)


def inverse(normal, eye, ex):
    top = jnp.max(jnp.sum(jnp.abs(normal), axis=1, keepdims=True), axis=0, keepdims=True)
    scale = 2.0 / (top + TIKHONOV)
    ex[0:PAD] = eye - scale * normal
    ex[PAD : 2 * PAD] = scale * eye

    def turn(_, rho):
        both = ex[...]
        err = both[0:PAD]
        product = dot3(both, err)
        gain = 2.0 / (2.0 - rho * rho)
        ex[0:PAD] = gain * product[0:PAD] + (1.0 - gain) * eye
        ex[PAD : 2 * PAD] = gain * (both[PAD : 2 * PAD] + product[PAD : 2 * PAD])
        return 0.5 * rho * rho * gain

    lax.fori_loop(0, ROUNDS, turn, (top - TIKHONOV) / (top + TIKHONOV))

    def polish(_, carry):
        now = ex[PAD : 2 * PAD]
        left = eye - dot6(normal, now)
        ex[PAD : 2 * PAD] = now + dot3(now, left)
        return carry

    lax.fori_loop(0, 3, polish, 0)
    return ex[PAD : 2 * PAD]


def tables(z, end, next_to_end, pairs, ex, q_high, q_low, e_high, e_low):
    dates = lax.broadcasted_iota(jnp.int32, (PAD, pairs.shape[1]), 0)
    design = (dates == pairs[1:2, :]).astype(f32) - (dates == pairs[0:1, :]).astype(f32)
    design = design.astype(bf16)
    row = lax.broadcasted_iota(jnp.int32, (PAD, PAD), 0)
    col = lax.broadcasted_iota(jnp.int32, (PAD, PAD), 1)
    eye = (row == col).astype(f32)
    normal = lax.dot_general(design, design, (((1,), (1,)), ((), ())), preferred_element_type=f32)
    normal = normal + TIKHONOV * eye
    solved = inverse(normal, eye, ex)
    at_z = (row * 2731) >> 16
    rest = row - SHARE * at_z
    at_x = (rest * 43) >> 8
    date = 48 * at_x + 6 * at_z + (rest - 6 * at_x)
    offset = (date - col).astype(f32) / TEMPORAL_SIGMA
    weight = jnp.where(col < ND, jnp.exp(-0.5 * offset * offset), 0.0)
    smooth = weight / jnp.sum(weight, axis=1, keepdims=True)
    change = dot6((date == col).astype(f32) - smooth, solved)
    first = change.astype(bf16)
    rest = change - first.astype(f32)
    second = rest.astype(bf16)
    third = (rest - second.astype(f32)).astype(bf16)
    k = lax.broadcasted_iota(jnp.int32, (pairs.shape[1], LANES), 0)
    j = lax.broadcasted_iota(jnp.int32, (pairs.shape[1], LANES), 1)

    def held(at):
        pick = (k == 256 * (j >> 5) + 32 * at + (j & 31)).astype(f32).astype(bf16)
        mine = dot(design, pick).astype(bf16)
        return dot(first, mine) + (dot(second, mine) + dot(third, mine))

    def keep(q, high_ref, low_ref):
        high, low = two(q[0:ND])
        high_ref[...] = jnp.concatenate([high, high], axis=1)
        low_ref[...] = low

    keep(held(z), q_high, q_low)

    @pl.when(next_to_end)
    def _():
        keep(jnp.where(at_z[:, 0:LANES] == end, 0.0, held(end)), e_high, e_low)


def kernel(
    ifg, pairs, out, x_buf, y_buf, p_buf, s_buf, fin, fr, ex, q_high, q_low, e_high, e_low,
    x_send, x_recv, y_send, y_recv, s_send, s_recv, f_send, f_recv, h_send, h_recv, go_line, go_all,
):
    stack = lax.axis_index("stack")
    slab = lax.axis_index("rows")
    slabs = lax.axis_size("rows")
    x = stack // (2 * LINE)
    z = (stack // 2) % LINE
    core = stack % 2
    me = 2 * x + core
    mirror = LINE - 1 - z
    half = z // (LINE // 2)
    near = z * (1 - half) + mirror * half
    end = (LINE - 1) * half
    at_end, next_to_end = near == 0, near == 1

    def peer(owner):
        return {"stack": 2 * LINE * (owner // 2) + 2 * z + owner % 2}

    def remote(src, dst, send, recv, device):
        return pltpu.make_async_remote_copy(
            src_ref=src, dst_ref=dst, send_sem=send, recv_sem=recv,
            device_id=device, device_id_type=pl.DeviceIdType.MESH,
        )

    def landed(ref, sem):
        pltpu.make_async_copy(ref, ref, sem).wait()

    def onward(way):
        return {"stack": stack + 2 - 4 * way}

    below = {"rows": slab + 1}
    above = {"rows": slab - 1}
    has_left, has_right = z > 0, z < LINE - 1
    has_above, has_below = slab > 0, slab < slabs - 1
    seam_below, seam_above = slab == slabs // 2 - 1, slab == slabs // 2
    gate_below, gate_above = seam_below & (z == LINE - 1), seam_above & (z == 0)
    gate_to_below = {"stack": stack - 2 * (LINE - 1), "rows": slab + 1}
    gate_to_above = {"stack": stack + 2 * (LINE - 1), "rows": slab - 1}

    barrier = pltpu.get_barrier_semaphore()

    def signal(sem, device):
        pl.semaphore_signal(sem, inc=1, device_id=device, device_id_type=pl.DeviceIdType.MESH)

    for step in range(1, OWNERS):
        signal(barrier, peer((me + step) % OWNERS))
    count = OWNERS - 1
    for there, device in (
        (has_left, onward(1)),
        (has_right, onward(0)),
        (has_above & jnp.logical_not(seam_above), above),
        (has_below & jnp.logical_not(seam_below), below),
        (gate_above, gate_to_above),
        (gate_below, gate_to_below),
    ):
        pl.when(there)(functools.partial(signal, barrier, device))
        count = count + there.astype(jnp.int32)
    pl.semaphore_wait(barrier, count)

    def band(c):
        return (c // 2 + BANDS - 1) % BANDS

    def half_rows(c):
        return pl.ds(HALF * (c % 2), HALF)

    def x_piece(c, owner):
        rows = pl.ds(8 * band(c) + HALF * (c % 2), HALF)
        return ifg.at[:, rows, pl.ds(pl.multiple_of(LANES * owner, LANES), LANES)]

    def x_slot(c):
        return x_buf.at[c // 2, pl.ds(DEPTH * me, DEPTH), half_rows(c)]

    def spread(c, carry):
        for step in range(1, OWNERS):
            owner = (me + step) % OWNERS
            remote(x_piece(c, owner), x_slot(c), x_send.at[c], x_recv.at[c], peer(owner)).start()
        pltpu.make_async_copy(x_piece(c, me), x_slot(c), x_recv.at[c]).start()
        return carry

    def x_landed(c):
        landed(x_buf.at[c // 2, :, half_rows(c)], x_recv.at[c])

    def whole(c, device):
        return remote(
            x_buf.at[c // 2, :, half_rows(c)], y_buf.at[c // 2, :, half_rows(c)], y_send.at[c], y_recv.at[c], device
        )

    lax.fori_loop(0, AHEAD, spread, 0)

    def spread_next(c):
        @pl.when(2 * c + AHEAD < CHUNKS)
        def _():
            spread(2 * c + AHEAD, 0)
            spread(2 * c + AHEAD + 1, 0)

    @pl.when(at_end)
    def _():
        def pass_on(c, carry):
            x_landed(c)
            whole(c, onward(half)).start()
            spread_next(c)
            return carry

        lax.fori_loop(0, WHOLE, pass_on, 0)

    tables(z, end, next_to_end, pairs, ex, q_high, q_low, e_high, e_low)

    @pl.when(jnp.logical_not(has_above))
    def _():
        fr[0] = jnp.zeros(fr.shape[1:], f32)

    @pl.when(jnp.logical_not(has_below))
    def _():
        fr[BANDS + 1] = jnp.zeros(fr.shape[1:], f32)

    taps = spatial_taps()

    def multiply(c, source, high_ref, low_ref, more):
        for s in range(0, HALF, 2):
            at = HALF * (c % 2) + s
            block = jnp.concatenate([source[c // 2, :, at], source[c // 2, :, at + 1]], axis=1)
            high, low = two(block)
            product = dot(high_ref[...], jnp.concatenate([high, low], axis=0)) + dot(low_ref[...], high)
            for t in range(2):
                part = product[:, LANES * t : LANES * (t + 1)].reshape(LINE, SHARE, LANES)
                p_buf[c, :, s + t] = part + p_buf[c, :, s + t] if more else part

    def compute(c):
        @pl.when(jnp.logical_not(at_end & (c < WHOLE)))
        def _():
            x_landed(c)
            spread_next(c)

        multiply(c, x_buf, q_high, q_low, False)

        @pl.when(next_to_end & (c < WHOLE))
        def _():
            landed(y_buf.at[c // 2, :, half_rows(c)], y_recv.at[c])
            multiply(c, y_buf, e_high, e_low, True)

    def low_pass(q):
        lane = lax.broadcasted_iota(jnp.int32, (8, LANES * OWNERS), 1)
        for i in range(KEEP):
            window = jnp.concatenate(
                [fr[q, :, i, 8 - R : 8], fr[q + 1, :, i], fr[q + 2, :, i, 0:R]], axis=1
            )
            rowpass = taps[R] * window[:, R : R + 8]
            for s in range(1, R + 1):
                rowpass = rowpass + taps[R + s] * (
                    window[:, R - s : R - s + 8] + window[:, R + s : R + s + 8]
                )
            line = jnp.concatenate([rowpass[o] for o in range(OWNERS)], axis=1)
            total = taps[R] * line
            width = LANES * OWNERS
            for s in range(1, R + 1):
                before = jnp.where(lane >= s, pltpu.roll(line, s, 1), 0.0)
                after = jnp.where(lane < width - s, pltpu.roll(line, width - s, 1), 0.0)
                total = total + taps[R + s] * (before + after)
            out[i, pl.ds(pl.multiple_of(8 * q, 8), 8)] = total

    halo_down = remote(
        fr.at[BANDS, :, :, pl.ds(8 - R, R)], fr.at[0, :, :, pl.ds(8 - R, R)], h_send.at[0], h_recv.at[0], below
    )
    halo_up = remote(
        fr.at[1, :, :, pl.ds(0, R)], fr.at[BANDS + 1, :, :, pl.ds(0, R)], h_send.at[1], h_recv.at[1], above
    )

    def finish(b):
        landed(fr.at[band(2 * b) + 1], f_recv.at[b])

        @pl.when((b == 0) & has_below & jnp.logical_not(seam_below))
        def _():
            halo_down.start()

        @pl.when((b == 1) & has_above & jnp.logical_not(seam_above))
        def _():
            halo_up.start()

        @pl.when((b == 2) & seam_below)
        def _():
            pl.when(has_right)(functools.partial(pl.semaphore_wait, go_all, 1))
            halo_down.start()

        @pl.when((b == 2) & seam_above)
        def _():
            pl.when(has_left)(functools.partial(pl.semaphore_wait, go_all, 1))
            halo_up.start()

        @pl.when(b >= 3)
        def _():
            low_pass(b - 2)

    def collect(c):
        for s in range(HALF):
            fin[c // 2, :, HALF * (c % 2) + s] = p_buf[c, z, s]

        @pl.when(c % 2 == 1)
        def _():
            b = c // 2
            slot = fr.at[band(c) + 1, me]
            for step in range(1, OWNERS):
                owner = (me + step) % OWNERS
                remote(fin.at[b, pl.ds(KEEP * owner, KEEP)], slot, f_send.at[b], f_recv.at[b], peer(owner)).start()
            pltpu.make_async_copy(fin.at[b, pl.ds(KEEP * me, KEEP)], slot, f_recv.at[b]).start()

            for gate, across, way in ((gate_below, gate_to_below, 1), (gate_above, gate_to_above, -1)):
                pl.when(gate & (b == 0))(functools.partial(signal, go_line, across))

                @pl.when(gate & (b == 1))
                def _():
                    pl.semaphore_wait(go_line, 1)
                    for hops in range(1, LINE):
                        signal(go_all, {"stack": stack - 2 * hops * way})

            @pl.when((b >= 1) & (b <= WHOLE // 2))
            def _():
                finish(b - 1)

    items = (LINE - 1) * CHUNKS
    first = (LINE - 1) * WHOLE

    def place(item):
        late = (item >= first).astype(jnp.int32)
        c = (item * 9363) >> 16
        after = item - first
        return (
            late * (WHOLE + (after & 7)) + (1 - late) * c,
            late * (after >> 3) + (1 - late) * (item - (LINE - 1) * c),
        )

    def flow(t, p, way, ends):
        item = t - LAG * p

        @pl.when((item >= 0) & (item < items))
        def _():
            c, hop = place(item)
            left_over = LINE - 1 - hop - p
            d = way * hop + (1 - way) * (LINE - 1 - hop)
            plain = c >= WHOLE

            @pl.when((ends == 0) & (hop == 0))
            def _():
                compute(c)

            @pl.when(left_over >= 0)
            def _():
                @pl.when((p > 1) | ((p == 1) & plain))
                def _():
                    landed(s_buf.at[way, c, d], s_recv.at[way, c, d])
                    p_buf[c, d] = p_buf[c, d] + s_buf[way, c, d]

                @pl.when((left_over > 0) & ((p > 0) | plain))
                def _():
                    remote(
                        p_buf.at[c, d], s_buf.at[way, c, d], s_send.at[way, c, d], s_recv.at[way, c, d], onward(way)
                    ).start()

                @pl.when((left_over == 0) & ((jnp.logical_not(plain) | at_end) if ends else plain))
                def _():
                    collect(c)

    def step(t, carry):
        flow(t, near, half, 0)
        flow(t, LINE - 1 - near, 1 - half, 1)
        return carry

    steps = max(items + LAG, first + CHUNKS - WHOLE + (LINE - 1) * LAG)
    lax.fori_loop(0, steps, step, 0)

    def rest(b, carry):
        finish(b)
        return carry

    lax.fori_loop(WHOLE // 2, BANDS, rest, 0)

    @pl.when(has_above)
    def _():
        halo_down.wait_recv()
        halo_up.wait_send()

    @pl.when(has_below)
    def _():
        halo_up.wait_recv()
        halo_down.wait_send()

    def tail(q, carry):
        low_pass(q)
        return carry

    low_pass(0)
    lax.fori_loop(BANDS - 2, BANDS, tail, 0)

    def drain(c, carry):
        landed(x_buf.at[0, pl.ds(0, (OWNERS - 1) * DEPTH), pl.ds(0, HALF)], x_send.at[c])
        head = at_end & (c < WHOLE)

        @pl.when(head)
        def _():
            landed(x_buf.at[0, :, pl.ds(0, HALF)], y_send.at[c])

        def each(d, carry):
            @pl.when((d > z) & jnp.logical_not((z == 0) & head))
            def _():
                landed(p_buf.at[c, d], s_send.at[0, c, d])

            @pl.when((d < z) & jnp.logical_not((mirror == 0) & head))
            def _():
                landed(p_buf.at[c, d], s_send.at[1, c, d])

            return carry

        return lax.fori_loop(0, LINE, each, carry)

    lax.fori_loop(0, CHUNKS, drain, 0)

    def drain_bands(b, carry):
        landed(fr.at[1, pl.ds(0, OWNERS - 1)], f_send.at[b])
        return carry

    lax.fori_loop(0, BANDS, drain_bands, 0)


def shards(interferograms, pairs):
    dma = pltpu.SemaphoreType.DMA
    block = (CHUNKS, LINE, HALF, SHARE, LANES)
    held = (BANDS, DEPTH * OWNERS, 8, LANES)
    return pl.pallas_call(
        kernel,
        out_shape=jax.ShapeDtypeStruct((KEEP,) + interferograms.shape[1:], f32),
        in_specs=[pl.BlockSpec(memory_space=pltpu.HBM), pl.BlockSpec(memory_space=pltpu.VMEM)],
        out_specs=pl.BlockSpec(memory_space=pltpu.VMEM),
        scratch_shapes=[
            pltpu.VMEM(held, f32),
            pltpu.VMEM((WHOLE // 2,) + held[1:], f32),
            pltpu.VMEM(block, f32),
            pltpu.VMEM((2,) + block, f32),
            pltpu.VMEM((BANDS, SHARE, 8, LANES), f32),
            pltpu.VMEM((BANDS + 2, OWNERS, KEEP, 8, LANES), f32),
            pltpu.VMEM((2 * PAD, PAD), f32),
            pltpu.VMEM((ND, 2 * LANES), bf16),
            pltpu.VMEM((ND, LANES), bf16),
            pltpu.VMEM((ND, 2 * LANES), bf16),
            pltpu.VMEM((ND, LANES), bf16),
            dma((CHUNKS,)), dma((CHUNKS,)),
            dma((WHOLE,)), dma((WHOLE,)),
            dma((2, CHUNKS, LINE)), dma((2, CHUNKS, LINE)),
            dma((BANDS,)), dma((BANDS,)),
            dma((2,)), dma((2,)),
            pltpu.SemaphoreType.REGULAR, pltpu.SemaphoreType.REGULAR,
        ],
        compiler_params=pltpu.CompilerParams(
            collective_id=0, has_side_effects=True, vmem_limit_bytes=61 * 1024 * 1024
        ),
    )(interferograms, pairs.T)


def solution(mesh):
    return jax.shard_map(
        shards,
        mesh=mesh,
        in_specs=(P("stack", "rows", None), P()),
        out_specs=P("stack", "rows", None),
        check_vma=False,
    )
```

time: 169 us -> 142 us (0.84)
  the two profiles are of different devices: /device:TPU:25 before, /device:TPU:65 now
where the time goes in v2:
time: 142 us
  Pallas kernels  140 us (99%)
  local copies, waits for them, and re-layouts  2.09 us (1%)
    pallas_call x1, Pallas kernels, shards(): pl.pallas_call(kernel, out_shape=jax.ShapeDtypeStruct((KEEP,) + interfero...  140 us

profile of v2, /device:TPU:65, one launch (start us, length us, event | category | flops | bytes accessed | tf_op | source)
XLA Modules:
  0.0 142.1 jit_solution(2924008202653408548)
XLA Ops:
  0.0 140.0 %shard_map.28 = f32[3,64,1024]{2,1,0:T(8,128)} custom-call(f32[16,64,1024]{2,1,0:T(8,128)} %ifg.1, s32[2,1024]{1,0:T(2,128)} %bitcast.1), custom_call_target="tpu_custom_call" | custom-call | tf_op jit(solution)/shard_map/pallas_call | solution.py:457
  140.1 2.1 %copy.4 = f32[3,64,1024]{2,1,0:T(8,128)} copy(f32[3,64,1024]{2,1,0:T(8,128)} %shard_map.28) | data formatting | bytes 1572864

commit v3 on v2

--- a/solution.py
+++ b/solution.py
@@ -27,6 +27,7 @@
 WHOLE = 8
 LAG = 6
 AHEAD = 4
+DIRECT = 2
 ROUNDS = 9
 f32 = jnp.float32
 bf16 = jnp.bfloat16
@@ -172,9 +173,21 @@
     def signal(sem, device):
         pl.semaphore_signal(sem, inc=1, device_id=device, device_id_type=pl.DeviceIdType.MESH)
 
+    def beside(owner, way):
+        return {"stack": 2 * LINE * (owner // 2) + 2 * (z + 1 - 2 * way) + owner % 2}
+
     for step in range(1, OWNERS):
         signal(barrier, peer((me + step) % OWNERS))
     count = OWNERS - 1
+    ends_pair = at_end | next_to_end
+    pair_way = half * at_end.astype(jnp.int32) + (1 - half) * next_to_end.astype(jnp.int32)
+
+    @pl.when(ends_pair)
+    def _():
+        for step in range(1, OWNERS):
+            signal(barrier, beside((me + step) % OWNERS, pair_way))
+
+    count = count + (OWNERS - 1) * ends_pair.astype(jnp.int32)
     for there, device in (
         (has_left, onward(1)),
         (has_right, onward(0)),
@@ -203,7 +216,7 @@
     def spread(c, carry):
         for step in range(1, OWNERS):
             owner = (me + step) % OWNERS
-            remote(x_piece(c, owner), x_slot(c), x_send.at[c], x_recv.at[c], peer(owner)).start()
+            remote(x_piece(c, owner), x_slot(c), x_send, x_recv.at[c], peer(owner)).start()
         pltpu.make_async_copy(x_piece(c, me), x_slot(c), x_recv.at[c]).start()
         return carry
 
@@ -212,8 +225,19 @@
 
     def whole(c, device):
         return remote(
-            x_buf.at[c // 2, :, half_rows(c)], y_buf.at[c // 2, :, half_rows(c)], y_send.at[c], y_recv.at[c], device
+            x_buf.at[c // 2, :, half_rows(c)], y_buf.at[c // 2, :, half_rows(c)], y_send, y_recv.at[c], device
         )
+
+    def spread_direct(c, carry):
+        for step in range(OWNERS):
+            owner = (me + step) % OWNERS
+            slot = y_buf.at[c // 2, pl.ds(DEPTH * me, DEPTH), half_rows(c)]
+            remote(x_piece(c, owner), slot, y_send, y_recv.at[c], beside(owner, half)).start()
+        return carry
+
+    @pl.when(at_end)
+    def _():
+        lax.fori_loop(0, DIRECT, spread_direct, 0)
 
     lax.fori_loop(0, AHEAD, spread, 0)
 
@@ -227,7 +251,11 @@
     def _():
         def pass_on(c, carry):
             x_landed(c)
-            whole(c, onward(half)).start()
+
+            @pl.when(c >= DIRECT)
+            def _():
+                whole(c, onward(half)).start()
+
             spread_next(c)
             return carry
 
@@ -330,7 +358,7 @@
             slot = fr.at[band(c) + 1, me]
             for step in range(1, OWNERS):
                 owner = (me + step) % OWNERS
-                remote(fin.at[b, pl.ds(KEEP * owner, KEEP)], slot, f_send.at[b], f_recv.at[b], peer(owner)).start()
+                remote(fin.at[b, pl.ds(KEEP * owner, KEEP)], slot, f_send, f_recv.at[b], peer(owner)).start()
             pltpu.make_async_copy(fin.at[b, pl.ds(KEEP * me, KEEP)], slot, f_recv.at[b]).start()
 
             for gate, across, way in ((gate_below, gate_to_below, 1), (gate_above, gate_to_above, -1)):
@@ -376,13 +404,13 @@
             def _():
                 @pl.when((p > 1) | ((p == 1) & plain))
                 def _():
-                    landed(s_buf.at[way, c, d], s_recv.at[way, c, d])
+                    landed(s_buf.at[way, c, d], s_recv.at[way, c, hop])
                     p_buf[c, d] = p_buf[c, d] + s_buf[way, c, d]
 
                 @pl.when((left_over > 0) & ((p > 0) | plain))
                 def _():
                     remote(
-                        p_buf.at[c, d], s_buf.at[way, c, d], s_send.at[way, c, d], s_recv.at[way, c, d], onward(way)
+                        p_buf.at[c, d], s_buf.at[way, c, d], s_send.at[way], s_recv.at[way, c, hop], onward(way)
                     ).start()
 
                 @pl.when((left_over == 0) & ((jnp.logical_not(plain) | at_end) if ends else plain))
@@ -420,34 +448,14 @@
     low_pass(0)
     lax.fori_loop(BANDS - 2, BANDS, tail, 0)
 
-    def drain(c, carry):
-        landed(x_buf.at[0, pl.ds(0, (OWNERS - 1) * DEPTH), pl.ds(0, HALF)], x_send.at[c])
-        head = at_end & (c < WHOLE)
-
-        @pl.when(head)
-        def _():
-            landed(x_buf.at[0, :, pl.ds(0, HALF)], y_send.at[c])
-
-        def each(d, carry):
-            @pl.when((d > z) & jnp.logical_not((z == 0) & head))
-            def _():
-                landed(p_buf.at[c, d], s_send.at[0, c, d])
-
-            @pl.when((d < z) & jnp.logical_not((mirror == 0) & head))
-            def _():
-                landed(p_buf.at[c, d], s_send.at[1, c, d])
-
-            return carry
-
-        return lax.fori_loop(0, LINE, each, carry)
-
-    lax.fori_loop(0, CHUNKS, drain, 0)
-
-    def drain_bands(b, carry):
-        landed(fr.at[1, pl.ds(0, OWNERS - 1)], f_send.at[b])
-        return carry
-
-    lax.fori_loop(0, BANDS, drain_bands, 0)
+    landed(x_buf.at[:, pl.ds(0, (OWNERS - 1) * DEPTH)], x_send)
+    landed(fr.at[pl.ds(1, BANDS), pl.ds(0, OWNERS - 1)], f_send)
+    pl.when(at_end)(functools.partial(landed, y_buf, y_send))
+    for way, p in ((0, z), (1, mirror)):
+        for k in range(LINE - 1):
+            chunks = pl.ds(0, CHUNKS) if k else pl.ds(WHOLE, CHUNKS - WHOLE)
+            ahead = p_buf.at[chunks, pl.ds(0, LINE - 1 - k)]
+            pl.when(p == k)(functools.partial(landed, ahead, s_send.at[way]))
 
 
 def shards(interferograms, pairs):
@@ -456,7 +464,7 @@
     held = (BANDS, DEPTH * OWNERS, 8, LANES)
     return pl.pallas_call(
         kernel,
-        out_shape=jax.ShapeDtypeStruct((KEEP,) + interferograms.shape[1:], f32),
+        out_shape=pltpu.VMEM((KEEP,) + interferograms.shape[1:], f32),
         in_specs=[pl.BlockSpec(memory_space=pltpu.HBM), pl.BlockSpec(memory_space=pltpu.VMEM)],
         out_specs=pl.BlockSpec(memory_space=pltpu.VMEM),
         scratch_shapes=[
@@ -471,10 +479,10 @@
             pltpu.VMEM((ND, LANES), bf16),
             pltpu.VMEM((ND, 2 * LANES), bf16),
             pltpu.VMEM((ND, LANES), bf16),
-            dma((CHUNKS,)), dma((CHUNKS,)),
-            dma((WHOLE,)), dma((WHOLE,)),
-            dma((2, CHUNKS, LINE)), dma((2, CHUNKS, LINE)),
-            dma((BANDS,)), dma((BANDS,)),
+            dma, dma((CHUNKS,)),
+            dma, dma((WHOLE,)),
+            dma((2,)), dma((2, CHUNKS, LINE - 1)),
+            dma, dma((BANDS,)),
             dma((2,)), dma((2,)),
             pltpu.SemaphoreType.REGULAR, pltpu.SemaphoreType.REGULAR,
         ],

time: 142 us -> 132 us (0.930)
  Pallas kernels: 140 us -> 131 us
    pallas_call x1, Pallas kernels: 140 us -> 131 us  [shards(): pl.pallas_call(kernel, out_shape=pltpu.VMEM((KEEP,) + interferograms.shap...]
where the time goes in v3:
time: 132 us
  Pallas kernels  131 us (99%)
    pallas_call x1, Pallas kernels, shards(): pl.pallas_call(kernel, out_shape=pltpu.VMEM((KEEP,) + interferograms.shap...  131 us

profile of v3, /device:TPU:65, one launch (start us, length us, event | category | flops | bytes accessed | tf_op | source)
XLA Modules:
  0.0 131.5 jit_solution(3699691719954199168)
XLA Ops:
  0.0 130.6 %shard_map.28 = f32[3,64,1024]{2,1,0:T(8,128)S(1)} custom-call(f32[16,64,1024]{2,1,0:T(8,128)} %ifg.1, s32[2,1024]{1,0:T(2,128)} %bitcast.1), custom_call_target="tpu_custom_call" | custom-call | tf_op jit(solution)/shard_map/pallas_call | solution.py:465
  130.6 0.9 copy.4

commit v4 on v3

--- a/solution.py
+++ b/solution.py
@@ -21,6 +21,7 @@
 BANDS = 8
 CHUNKS = 16
 HALF = 4
+UNITS = 9
 SHARE = ND // LINE
 KEEP = ND // (LINE * OWNERS)
 PAD = 256
@@ -85,15 +86,19 @@
     return ex[PAD : 2 * PAD]
 
 
-def tables(z, end, next_to_end, pairs, ex, q_high, q_low, e_high, e_low):
+def network(pairs):
     dates = lax.broadcasted_iota(jnp.int32, (PAD, pairs.shape[1]), 0)
     design = (dates == pairs[1:2, :]).astype(f32) - (dates == pairs[0:1, :]).astype(f32)
     design = design.astype(bf16)
+    return design, lax.dot_general(design, design, (((1,), (1,)), ((), ())), preferred_element_type=f32)
+
+
+def tables(z, end, next_to_end, pairs, design_ref, ex, q_high, q_low, e_high, e_low):
+    design = design_ref[...]
     row = lax.broadcasted_iota(jnp.int32, (PAD, PAD), 0)
     col = lax.broadcasted_iota(jnp.int32, (PAD, PAD), 1)
     eye = (row == col).astype(f32)
-    normal = lax.dot_general(design, design, (((1,), (1,)), ((), ())), preferred_element_type=f32)
-    normal = normal + TIKHONOV * eye
+    normal = ex[0:PAD] + TIKHONOV * eye
     solved = inverse(normal, eye, ex)
     at_z = (row * 2731) >> 16
     rest = row - SHARE * at_z
@@ -128,7 +133,7 @@
 
 
 def kernel(
-    ifg, pairs, out, x_buf, y_buf, p_buf, s_buf, fin, fr, ex, q_high, q_low, e_high, e_low,
+    ifg, pairs, out, x_buf, y_buf, p_buf, s_buf, fin, fr, design_ref, ex, q_high, q_low, e_high, e_low,
     x_send, x_recv, y_send, y_recv, s_send, s_recv, f_send, f_recv, h_send, h_recv, go_line, go_all,
 ):
     stack = lax.axis_index("stack")
@@ -198,6 +203,7 @@
     ):
         pl.when(there)(functools.partial(signal, barrier, device))
         count = count + there.astype(jnp.int32)
+    design_ref[...], ex[0:PAD] = network(pairs)
     pl.semaphore_wait(barrier, count)
 
     def band(c):
@@ -225,19 +231,23 @@
 
     def whole(c, device):
         return remote(
-            x_buf.at[c // 2, :, half_rows(c)], y_buf.at[c // 2, :, half_rows(c)], y_send, y_recv.at[c], device
+            x_buf.at[c // 2, :, half_rows(c)], y_buf.at[c // 2, :, half_rows(c)], y_send, y_recv.at[c + 1], device
         )
 
-    def spread_direct(c, carry):
+    def spread_direct(unit, band_row, height):
         for step in range(OWNERS):
             owner = (me + step) % OWNERS
-            slot = y_buf.at[c // 2, pl.ds(DEPTH * me, DEPTH), half_rows(c)]
-            remote(x_piece(c, owner), slot, y_send, y_recv.at[c], beside(owner, half)).start()
-        return carry
+            piece = ifg.at[
+                :, pl.ds(8 * band(0) + band_row, height), pl.ds(pl.multiple_of(LANES * owner, LANES), LANES)
+            ]
+            slot = y_buf.at[0, pl.ds(DEPTH * me, DEPTH), pl.ds(band_row, height)]
+            remote(piece, slot, y_send, y_recv.at[unit], beside(owner, half)).start()
 
     @pl.when(at_end)
     def _():
-        lax.fori_loop(0, DIRECT, spread_direct, 0)
+        spread_direct(0, 0, HALF // 2)
+        spread_direct(1, HALF // 2, HALF // 2)
+        spread_direct(2, HALF, HALF)
 
     lax.fori_loop(0, AHEAD, spread, 0)
 
@@ -261,7 +271,7 @@
 
         lax.fori_loop(0, WHOLE, pass_on, 0)
 
-    tables(z, end, next_to_end, pairs, ex, q_high, q_low, e_high, e_low)
+    tables(z, end, next_to_end, pairs, design_ref, ex, q_high, q_low, e_high, e_low)
 
     @pl.when(jnp.logical_not(has_above))
     def _():
@@ -273,8 +283,8 @@
 
     taps = spatial_taps()
 
-    def multiply(c, source, high_ref, low_ref, more):
-        for s in range(0, HALF, 2):
+    def multiply(c, source, high_ref, low_ref, more, rows=range(0, HALF, 2)):
+        for s in rows:
             at = HALF * (c % 2) + s
             block = jnp.concatenate([source[c // 2, :, at], source[c // 2, :, at + 1]], axis=1)
             high, low = two(block)
@@ -291,10 +301,13 @@
 
         multiply(c, x_buf, q_high, q_low, False)
 
-        @pl.when(next_to_end & (c < WHOLE))
-        def _():
-            landed(y_buf.at[c // 2, :, half_rows(c)], y_recv.at[c])
-            multiply(c, y_buf, e_high, e_low, True)
+    def compute_end(c):
+        landed(y_buf.at[c // 2, :, half_rows(c)], y_recv.at[c + 1])
+        multiply(c, y_buf, e_high, e_low, True)
+
+    def compute_part(unit):
+        landed(y_buf.at[0, :, pl.ds(HALF // 2 * unit, HALF // 2)], y_recv.at[unit])
+        multiply(0, y_buf, e_high, e_low, True, (HALF // 2 * unit,))
 
     def low_pass(q):
         lane = lax.broadcasted_iota(jnp.int32, (8, LANES * OWNERS), 1)
@@ -374,16 +387,19 @@
             def _():
                 finish(b - 1)
 
-    items = (LINE - 1) * CHUNKS
-    first = (LINE - 1) * WHOLE
+    items = (LINE - 1) * (CHUNKS + 1)
+    first = (LINE - 1) * UNITS
 
     def place(item):
         late = (item >= first).astype(jnp.int32)
-        c = (item * 9363) >> 16
+        unit = (item * 9363) >> 16
         after = item - first
+        head = (unit > 0).astype(jnp.int32)
         return (
-            late * (WHOLE + (after & 7)) + (1 - late) * c,
-            late * (after >> 3) + (1 - late) * (item - (LINE - 1) * c),
+            late * (WHOLE + (after & 7)) + (1 - late) * (unit - head),
+            late * (after >> 3) + (1 - late) * (item - (LINE - 1) * unit),
+            late * (UNITS + (after & 7)) + (1 - late) * unit,
+            late * (after & 7) + (1 - late) * unit,
         )
 
     def flow(t, p, way, ends):
@@ -391,29 +407,49 @@
 
         @pl.when((item >= 0) & (item < items))
         def _():
-            c, hop = place(item)
+            c, hop, unit, turn = place(item)
             left_over = LINE - 1 - hop - p
             d = way * hop + (1 - way) * (LINE - 1 - hop)
             plain = c >= WHOLE
 
-            @pl.when((ends == 0) & (hop == 0))
-            def _():
-                compute(c)
+            if ends == 0:
+
+                @pl.when(hop == 0)
+                def _():
+                    pl.when(unit != 1)(functools.partial(compute, c))
+
+                    @pl.when(next_to_end)
+                    def _():
+                        pl.when(unit == 0)(functools.partial(compute_part, 0))
+                        pl.when(unit == 1)(functools.partial(compute_part, 1))
+                        pl.when((unit > 1) & (c < WHOLE))(functools.partial(compute_end, c))
+
+            def travel(rows):
+                @pl.when((p > 1) | ((p == 1) & plain))
+                def _():
+                    landed(s_buf.at[way, c, d, rows], s_recv.at[way, turn, hop])
+                    p_buf[c, d, rows] = p_buf[c, d, rows] + s_buf[way, c, d, rows]
+
+                @pl.when((left_over > 0) & ((p > 0) | plain))
+                def _():
+                    remote(
+                        p_buf.at[c, d, rows], s_buf.at[way, c, d, rows], s_send.at[way], s_recv.at[way, turn, hop],
+                        onward(way),
+                    ).start()
 
             @pl.when(left_over >= 0)
             def _():
-                @pl.when((p > 1) | ((p == 1) & plain))
-                def _():
-                    landed(s_buf.at[way, c, d], s_recv.at[way, c, hop])
-                    p_buf[c, d] = p_buf[c, d] + s_buf[way, c, d]
-
-                @pl.when((left_over > 0) & ((p > 0) | plain))
-                def _():
-                    remote(
-                        p_buf.at[c, d], s_buf.at[way, c, d], s_send.at[way], s_recv.at[way, c, hop], onward(way)
-                    ).start()
-
-                @pl.when((left_over == 0) & ((jnp.logical_not(plain) | at_end) if ends else plain))
+                @pl.when(unit < 2)
+                def _():
+                    travel(pl.ds(HALF // 2 * unit, HALF // 2))
+
+                @pl.when(unit >= 2)
+                def _():
+                    travel(pl.ds(0, HALF))
+
+                last = (left_over == 0) & (unit > 0)
+
+                @pl.when(last & ((jnp.logical_not(plain) | at_end) if ends else plain))
                 def _():
                     collect(c)
 
@@ -429,7 +465,7 @@
         finish(b)
         return carry
 
-    lax.fori_loop(WHOLE // 2, BANDS, rest, 0)
+    lax.fori_loop(WHOLE // 2, BANDS - 1, rest, 0)
 
     @pl.when(has_above)
     def _():
@@ -440,12 +476,14 @@
     def _():
         halo_up.wait_recv()
         halo_down.wait_send()
+
+    low_pass(0)
+    finish(BANDS - 1)
 
     def tail(q, carry):
         low_pass(q)
         return carry
 
-    low_pass(0)
     lax.fori_loop(BANDS - 2, BANDS, tail, 0)
 
     landed(x_buf.at[:, pl.ds(0, (OWNERS - 1) * DEPTH)], x_send)
@@ -474,14 +512,15 @@
             pltpu.VMEM((2,) + block, f32),
             pltpu.VMEM((BANDS, SHARE, 8, LANES), f32),
             pltpu.VMEM((BANDS + 2, OWNERS, KEEP, 8, LANES), f32),
+            pltpu.VMEM((PAD, 1024), bf16),
             pltpu.VMEM((2 * PAD, PAD), f32),
             pltpu.VMEM((ND, 2 * LANES), bf16),
             pltpu.VMEM((ND, LANES), bf16),
             pltpu.VMEM((ND, 2 * LANES), bf16),
             pltpu.VMEM((ND, LANES), bf16),
             dma, dma((CHUNKS,)),
-            dma, dma((WHOLE,)),
-            dma((2,)), dma((2, CHUNKS, LINE - 1)),
+            dma, dma((UNITS,)),
+            dma((2,)), dma((2, UNITS, LINE - 1)),
             dma, dma((BANDS,)),
             dma((2,)), dma((2,)),
             pltpu.SemaphoreType.REGULAR, pltpu.SemaphoreType.REGULAR,

time: 132 us -> 130 us (0.985)
  Pallas kernels: 131 us -> 129 us
    pallas_call x1, Pallas kernels: 131 us -> 129 us  [shards(): pl.pallas_call(kernel, out_shape=pltpu.VMEM((KEEP,) + interferograms.shap...]
where the time goes in v4:
time: 130 us
  Pallas kernels  129 us (99%)
    pallas_call x1, Pallas kernels, shards(): pl.pallas_call(kernel, out_shape=pltpu.VMEM((KEEP,) + interferograms.shap...  129 us

profile of v4, /device:TPU:65, one launch (start us, length us, event | category | flops | bytes accessed | tf_op | source)
XLA Modules:
  0.0 130.1 jit_solution(15844769175136676622)
XLA Ops:
  0.0 129.2 %shard_map.28 = f32[3,64,1024]{2,1,0:T(8,128)S(1)} custom-call(f32[16,64,1024]{2,1,0:T(8,128)} %ifg.1, s32[2,1024]{1,0:T(2,128)} %bitcast.1), custom_call_target="tpu_custom_call" | custom-call | tf_op jit(solution)/shard_map/pallas_call | solution.py:503
  129.2 0.9 copy.4

commit v5 on v4

--- a/solution.py
+++ b/solution.py
@@ -27,7 +27,8 @@
 PAD = 256
 WHOLE = 8
 LAG = 6
-AHEAD = 4
+RELAY = 95
+AHEAD = 6
 DIRECT = 2
 ROUNDS = 9
 f32 = jnp.float32
@@ -134,7 +135,7 @@
 
 def kernel(
     ifg, pairs, out, x_buf, y_buf, p_buf, s_buf, fin, fr, design_ref, ex, q_high, q_low, e_high, e_low,
-    x_send, x_recv, y_send, y_recv, s_send, s_recv, f_send, f_recv, h_send, h_recv, go_line, go_all,
+    x_send, x_recv, y_send, y_recv, s_send, s_recv, f_send, f_recv, h_send, h_recv, go_line, go_all, relay, relay_send, relay_recv,
 ):
     stack = lax.axis_index("stack")
     slab = lax.axis_index("rows")
@@ -336,6 +337,20 @@
         fr.at[1, :, :, pl.ds(0, R)], fr.at[BANDS + 1, :, :, pl.ds(0, R)], h_send.at[1], h_recv.at[1], above
     )
 
+    halfway = stack + 4 * 2 * (1 - 2 * half)
+    lower, upper = pl.ds(8 - R, R), pl.ds(0, R)
+    seam_down = remote(
+        fr.at[BANDS, :, :, lower], relay.at[:, :, lower], h_send.at[0], relay_recv, {"stack": halfway}
+    )
+    seam_down_on = remote(
+        relay.at[:, :, lower], fr.at[0, :, :, lower], relay_send, h_recv.at[0], {"stack": halfway, "rows": slab + 1}
+    )
+    seam_up = remote(fr.at[1, :, :, upper], relay.at[:, :, upper], h_send.at[1], relay_recv, {"stack": halfway})
+    seam_up_on = remote(
+        relay.at[:, :, upper], fr.at[BANDS + 1, :, :, upper], relay_send, h_recv.at[1],
+        {"stack": halfway, "rows": slab - 1},
+    )
+
     def finish(b):
         landed(fr.at[band(2 * b) + 1], f_recv.at[b])
 
@@ -347,15 +362,15 @@
         def _():
             halo_up.start()
 
-        @pl.when((b == 2) & seam_below)
+        @pl.when((b == 1) & seam_below)
         def _():
             pl.when(has_right)(functools.partial(pl.semaphore_wait, go_all, 1))
-            halo_down.start()
-
-        @pl.when((b == 2) & seam_above)
+            seam_down.start()
+
+        @pl.when((b == 1) & seam_above)
         def _():
             pl.when(has_left)(functools.partial(pl.semaphore_wait, go_all, 1))
-            halo_up.start()
+            seam_up.start()
 
         @pl.when(b >= 3)
         def _():
@@ -364,6 +379,14 @@
     def collect(c):
         for s in range(HALF):
             fin[c // 2, :, HALF * (c % 2) + s] = p_buf[c, z, s]
+
+        for gate, way in ((gate_below, 1), (gate_above, -1)):
+
+            @pl.when(gate & (c == 2))
+            def _():
+                pl.semaphore_wait(go_line, 1)
+                for hops in range(1, LINE):
+                    signal(go_all, {"stack": stack - 2 * hops * way})
 
         @pl.when(c % 2 == 1)
         def _():
@@ -374,14 +397,8 @@
                 remote(fin.at[b, pl.ds(KEEP * owner, KEEP)], slot, f_send, f_recv.at[b], peer(owner)).start()
             pltpu.make_async_copy(fin.at[b, pl.ds(KEEP * me, KEEP)], slot, f_recv.at[b]).start()
 
-            for gate, across, way in ((gate_below, gate_to_below, 1), (gate_above, gate_to_above, -1)):
+            for gate, across in ((gate_below, gate_to_below), (gate_above, gate_to_above)):
                 pl.when(gate & (b == 0))(functools.partial(signal, go_line, across))
-
-                @pl.when(gate & (b == 1))
-                def _():
-                    pl.semaphore_wait(go_line, 1)
-                    for hops in range(1, LINE):
-                        signal(go_all, {"stack": stack - 2 * hops * way})
 
             @pl.when((b >= 1) & (b <= WHOLE // 2))
             def _():
@@ -456,6 +473,14 @@
     def step(t, carry):
         flow(t, near, half, 0)
         flow(t, LINE - 1 - near, 1 - half, 1)
+
+        for there, first_leg, second_leg in ((seam_below, seam_down, seam_down_on), (seam_above, seam_up, seam_up_on)):
+
+            @pl.when(there & (t == RELAY))
+            def _():
+                first_leg.wait_recv()
+                second_leg.start()
+
         return carry
 
     steps = max(items + LAG, first + CHUNKS - WHOLE + (LINE - 1) * LAG)
@@ -485,6 +510,9 @@
         return carry
 
     lax.fori_loop(BANDS - 2, BANDS, tail, 0)
+
+    pl.when(seam_below)(seam_down_on.wait_send)
+    pl.when(seam_above)(seam_up_on.wait_send)
 
     landed(x_buf.at[:, pl.ds(0, (OWNERS - 1) * DEPTH)], x_send)
     landed(fr.at[pl.ds(1, BANDS), pl.ds(0, OWNERS - 1)], f_send)
@@ -524,6 +552,7 @@
             dma, dma((BANDS,)),
             dma((2,)), dma((2,)),
             pltpu.SemaphoreType.REGULAR, pltpu.SemaphoreType.REGULAR,
+            pltpu.VMEM((OWNERS, KEEP, 8, LANES), f32), dma, dma,
         ],
         compiler_params=pltpu.CompilerParams(
             collective_id=0, has_side_effects=True, vmem_limit_bytes=61 * 1024 * 1024

time: 130 us -> 129 us (level)
  no operation moved by 1% of the time
where the time goes in v5:
time: 129 us
  Pallas kernels  128 us (99%)
    pallas_call x1, Pallas kernels, shards(): pl.pallas_call(kernel, out_shape=pltpu.VMEM((KEEP,) + interferograms.shap...  128 us

profile of v5, /device:TPU:65, one launch (start us, length us, event | category | flops | bytes accessed | tf_op | source)
XLA Modules:
  0.0 129.1 jit_solution(8820487222088909803)
XLA Ops:
  0.0 128.2 %shard_map.28 = f32[3,64,1024]{2,1,0:T(8,128)S(1)} custom-call(f32[16,64,1024]{2,1,0:T(8,128)} %ifg.1, s32[2,1024]{1,0:T(2,128)} %bitcast.1), custom_call_target="tpu_custom_call" | custom-call | tf_op jit(solution)/shard_map/pallas_call | solution.py:531
  128.2 0.9 copy.4

commit v6 on v5

--- a/solution.py
+++ b/solution.py
@@ -26,7 +26,7 @@
 KEEP = ND // (LINE * OWNERS)
 PAD = 256
 WHOLE = 8
-LAG = 6
+LAG = 7
 RELAY = 95
 AHEAD = 6
 DIRECT = 2
@@ -427,6 +427,7 @@
             c, hop, unit, turn = place(item)
             left_over = LINE - 1 - hop - p
             d = way * hop + (1 - way) * (LINE - 1 - hop)
+            row = hop + way * (LINE - 2 * hop)
             plain = c >= WHOLE
 
             if ends == 0:
@@ -444,13 +445,13 @@
             def travel(rows):
                 @pl.when((p > 1) | ((p == 1) & plain))
                 def _():
-                    landed(s_buf.at[way, c, d, rows], s_recv.at[way, turn, hop])
+                    landed(s_buf.at[way, c, d, rows], s_recv.at[turn, row])
                     p_buf[c, d, rows] = p_buf[c, d, rows] + s_buf[way, c, d, rows]
 
                 @pl.when((left_over > 0) & ((p > 0) | plain))
                 def _():
                     remote(
-                        p_buf.at[c, d, rows], s_buf.at[way, c, d, rows], s_send.at[way], s_recv.at[way, turn, hop],
+                        p_buf.at[c, d, rows], s_buf.at[way, c, d, rows], s_send.at[way], s_recv.at[turn, row],
                         onward(way),
                     ).start()
 
@@ -548,7 +549,7 @@
             pltpu.VMEM((ND, LANES), bf16),
             dma, dma((CHUNKS,)),
             dma, dma((UNITS,)),
-            dma((2,)), dma((2, UNITS, LINE - 1)),
+            dma((2,)), dma((UNITS, LINE + 1)),
             dma, dma((BANDS,)),
             dma((2,)), dma((2,)),
             pltpu.SemaphoreType.REGULAR, pltpu.SemaphoreType.REGULAR,

time: 129 us -> 129 us (level)
  no operation moved by 1% of the time
where the time goes in v6:
time: 129 us
  Pallas kernels  128 us (99%)
    pallas_call x1, Pallas kernels, shards(): pl.pallas_call(kernel, out_shape=pltpu.VMEM((KEEP,) + interferograms.shap...  128 us

profile of v6, /device:TPU:65, one launch (start us, length us, event | category | flops | bytes accessed | tf_op | source)
XLA Modules:
  0.0 128.7 jit_solution(11506263506333151415)
XLA Ops:
  0.0 127.8 %shard_map.28 = f32[3,64,1024]{2,1,0:T(8,128)S(1)} custom-call(f32[16,64,1024]{2,1,0:T(8,128)} %ifg.1, s32[2,1024]{1,0:T(2,128)} %bitcast.1), custom_call_target="tpu_custom_call" | custom-call | tf_op jit(solution)/shard_map/pallas_call | solution.py:532
  127.9 0.9 copy.4
